TPU v7x, 32 devices: a whole 2x2x4 slice. The times are simulated.
32 devices in a mesh: groups: 2 (over y), frames: 4 (over z), code: 2 (over x), head: 2 (over core).
Axes of the slice: x: 2, y: 2, z: 4, core: 2. Of those that a mesh axis runs over, the one named last changes fastest.
Arguments:
- video: bfloat16 [256, 16, 1024], P(('code', 'head'), ('groups', 'frames')), parts along dimension 1, may hold values from -6 to 6
- conv_weight: bfloat16 [3, 1024, 1024], replicated, may hold values from -0.109375 to 0.109375
- norm_gain: float32 [1024], replicated, may hold values from 0.1 to 1.9
- qkv_weight: bfloat16 [1024, 3, 1024], P(None, None, ('code', 'head')), may hold values from -1 to 1
- out_weight: bfloat16 [1024, 1024], P(('code', 'head')), may hold values from -0.1875 to 0.1875
- latent_weight: bfloat16 [1024, 16], replicated, may hold values from -0.1875 to 0.1875
- codebook: bfloat16 [16, 65536], P(None, ('code', 'head')), may hold values from -9 to 9
- reference_codes: int32 [256, 16], P(None, ('groups', 'frames')), parts along dimension 1, may hold values from 0 to 65535
Outputs:
- encoded: bfloat16 [256, 16, 1024], P(('code', 'head'), ('groups', 'frames')), parts along dimension 1
- nearest_distance: float32 [256, 16], P(('code', 'head'), ('groups', 'frames')), parts along dimension 1
- reference_gap: float32 [256, 16], P(('code', 'head'), ('groups', 'frames')), parts along dimension 1
There are 2 independent parts, one for each index of `groups`. A program takes and returns all parts, laid end to end along the dimension named above; an argument that names none is the same for every part. Nothing has to cross between parts.
All inputs are finite; a program needn't handle non-finite values.
Results may differ from a plain program's by a relative error of at most 0.015.
Values may be sent and summed in bfloat16 or wider, within the bound.
A program may use at most 64 MiB of HBM per device.

v0:
```python
import math

import jax
import jax.numpy as jnp
from jax import lax
from jax.sharding import PartitionSpec as P

HEADS = 16


EPSILON = 1e-06


def passed_along(block, axis, distance):
    devices = range(lax.axis_size(axis))
    route = [(i - distance, i) for i in devices if i - distance in devices]
    return lax.ppermute(block, axis, route)


def merged(value, axis, combine):
    everything = jax.tree.map(lambda part: lax.all_gather(part, axis), value)
    leading = jax.tree.map(lambda part: part[0], everything)

    def lap(k, so_far):
        return combine(so_far, jax.tree.map(lambda part: part[k], everything))

    return lax.fori_loop(1, lax.axis_size(axis), lap, leading)


def normalize(block_input, norm_gain):
    values32 = block_input.astype(jnp.float32)
    mean_square = jnp.mean(values32 * values32, axis=-1, keepdims=True)
    return (values32 * lax.rsqrt(mean_square + EPSILON) * norm_gain).astype(jnp.bfloat16)


def attend_slab(queries, query_frame, keys, values, frames_here, local_heads, head_dim):
    slab_rows = queries.shape[0]
    query_heads = queries.reshape(slab_rows, local_heads, head_dim)
    score_scale = 1.0 / math.sqrt(head_dim)
    latest = jnp.max(query_frame)
    start_state = (
        jnp.full((slab_rows, local_heads), -1e30, jnp.float32),
        jnp.zeros((slab_rows, local_heads), jnp.float32),
        jnp.zeros((slab_rows, local_heads, head_dim), jnp.float32),
    )
    running = start_state
    key_part = lax.all_gather(keys, "frames", axis=0, tiled=True)
    value_part = lax.all_gather(values, "frames", axis=0, tiled=True)
    length = key_part.shape[0]
    block = math.gcd(length, slab_rows)
    count = length // block
    key_blocks = key_part.reshape(count, block, local_heads, head_dim)
    value_blocks = value_part.reshape(count, block, local_heads, head_dim)

    def absorb_visit(state, operands):
        key_block, value_block, block_index = operands
        first_row = block_index * block

        def compute(current):
            highest, denominator, summed = current
            key_rows = first_row + jnp.arange(block, dtype=jnp.int32)
            key_frame = key_rows // slab_rows * frames_here + key_rows % frames_here
            allowed = (key_frame[None, :] <= query_frame[:, None])[:, None, :]
            scores = (
                jnp.einsum(
                    "qhd,khd->qhk", query_heads, key_block, preferred_element_type=jnp.float32
                )
                * score_scale
            )
            scores = jnp.where(allowed, scores, -1e30)
            fresh = jnp.maximum(highest, jnp.max(scores, axis=2))
            weights = jnp.where(allowed, jnp.exp(scores - fresh[:, :, None]), 0.0)
            factor = jnp.exp(highest - fresh)
            denominator = denominator * factor + jnp.sum(weights, axis=2)
            summed = summed * factor[:, :, None] + jnp.einsum(
                "qhk,khd->qhd",
                weights.astype(jnp.bfloat16),
                value_block,
                preferred_element_type=jnp.float32,
            )
            return (fresh, denominator, summed)

        earliest = first_row // slab_rows * frames_here
        state = lax.cond(earliest <= latest, compute, lambda kept: kept, state)
        return (state, None)

    running, unused = lax.scan(
        absorb_visit, running, (key_blocks, value_blocks, jnp.arange(count, dtype=jnp.int32))
    )
    highest, denominator, summed = running
    return (
        (summed / denominator[:, :, None])
        .reshape(slab_rows, local_heads * head_dim)
        .astype(jnp.bfloat16)
    )


def scan_codes(running, latent_t, codes, offset, wanted):
    code_dim, length = codes.shape
    block = math.gcd(length, 4096)
    count = length // block
    latent32 = latent_t.astype(jnp.float32)
    squares = jnp.sum(latent32 * latent32, axis=0)
    code_blocks = jnp.transpose(codes.reshape(code_dim, count, block), (1, 0, 2))

    def scan_visit(state, operands):
        least, chosen = state
        code_block, block_index = operands
        codes32 = code_block.astype(jnp.float32)
        code_squares = jnp.sum(codes32 * codes32, axis=0)
        dots = lax.dot_general(
            latent_t, code_block, (((0,), (0,)), ((), ())), preferred_element_type=jnp.float32
        )
        distance = (squares[:, None] - 2.0 * dots + code_squares[None, :]) / code_dim
        labels = offset + block_index * block + jnp.arange(block, dtype=jnp.int32)
        least = jnp.minimum(least, jnp.min(distance, axis=1))
        chosen = chosen + jnp.sum(
            jnp.where(labels[None, :] == wanted[:, None], distance, 0.0), axis=1
        )
        return ((least, chosen), None)

    running, unused = lax.scan(
        scan_visit, running, (code_blocks, jnp.arange(count, dtype=jnp.int32))
    )
    return running


def empty_state(count):
    return (jnp.full((count,), 1e30, jnp.float32), jnp.zeros((count,), jnp.float32))


def combine_minima(first, second):
    return (jnp.minimum(first[0], second[0]), first[1] + second[1])


def shards(
    video, conv_weight, norm_gain, qkv_weight, out_weight, latent_weight, codebook, reference_codes
):
    positions, frames_here, model_width = video.shape
    own_rows = positions * frames_here
    earlier = passed_along(video, "frames", 1)
    padded = jnp.concatenate([earlier, video], axis=1)
    stacked = jnp.concatenate([padded[:, 2:], padded[:, 1:-1], padded[:, :-2]], axis=2)
    mixed = jnp.dot(
        stacked.reshape(own_rows, 3 * model_width),
        conv_weight.reshape(3 * model_width, model_width),
        preferred_element_type=jnp.float32,
    )
    block_input = (
        video.reshape(own_rows, model_width).astype(jnp.float32) + jax.nn.silu(mixed)
    ).astype(jnp.bfloat16)
    normed = normalize(block_input, norm_gain)
    local_width = qkv_weight.shape[2]
    projection = qkv_weight.reshape(model_width, 3 * local_width)
    triple = jnp.dot(
        lax.all_gather(normed, ("code", "head"), axis=0, tiled=True),
        projection,
        preferred_element_type=jnp.float32,
    ).astype(jnp.bfloat16)
    queries = triple[:, :local_width]
    keys = triple[:, local_width : 2 * local_width]
    values = triple[:, 2 * local_width :]
    slab_rows = triple.shape[0]
    head_dim = model_width // HEADS
    local_heads = local_width // head_dim
    slab_index = lax.axis_index("frames")
    local_frame = jnp.arange(slab_rows, dtype=jnp.int32) % frames_here
    query_frame = slab_index * frames_here + local_frame
    attended = attend_slab(queries, query_frame, keys, values, frames_here, local_heads, head_dim)
    projected = lax.psum_scatter(
        jnp.dot(attended, out_weight, preferred_element_type=jnp.float32).astype(jnp.bfloat16),
        ("code", "head"),
        scatter_dimension=0,
        tiled=True,
    ).astype(jnp.float32)
    encoded_rows = (block_input.astype(jnp.float32) + projected).astype(jnp.bfloat16)
    encoded = encoded_rows.reshape(positions, frames_here, model_width)
    latent_t = lax.dot_general(
        latent_weight, encoded_rows, (((0,), (1,)), ((), ())), preferred_element_type=jnp.float32
    ).astype(jnp.bfloat16)
    group_index = lax.axis_index(("code", "head"))
    wanted_all = reference_codes.reshape(-1)
    every_latent = lax.all_gather(latent_t, ("code", "head"), axis=1, tiled=True)
    shard_codes = codebook.shape[1]
    partial_state = scan_codes(
        empty_state(every_latent.shape[1]),
        every_latent,
        codebook,
        group_index * shard_codes,
        wanted_all,
    )
    merged_least, merged_chosen = merged(partial_state, ("code", "head"), combine_minima)
    least = lax.dynamic_slice_in_dim(merged_least, group_index * own_rows, own_rows, 0)
    chosen = lax.dynamic_slice_in_dim(merged_chosen, group_index * own_rows, own_rows, 0)
    return (
        encoded,
        least.reshape(positions, frames_here),
        (chosen - least).reshape(positions, frames_here),
    )


def solution(mesh):
    return jax.shard_map(
        shards,
        mesh=mesh,
        in_specs=(
            P(("code", "head"), ("groups", "frames"), None),
            P(),
            P(),
            P(None, None, ("code", "head")),
            P(("code", "head"), None),
            P(),
            P(None, ("code", "head")),
            P(None, ("groups", "frames")),
        ),
        out_specs=(
            P(("code", "head"), ("groups", "frames"), None),
            P(("code", "head"), ("groups", "frames")),
            P(("code", "head"), ("groups", "frames")),
        ),
        check_vma=False,
    )
```

profile of v0, /device:TPU:16, one launch (start us, length us, event | category | flops | bytes accessed | tf_op | source)
XLA Modules:
  0.0 230.6 jit_solution(13557342944345085490)
XLA Ops:
  7.2 3.6 %collective-permute-start = (bf16[64,2,1024]{2,1,0:T(2,128)(2,1)}, bf16[64,2,1024]{2,1,0:T(2,128)(2,1)S(1)}, u32[]{:S(2)}, u32[]{:S(2)}) collective-permute-start(bf16[64,2,1024]{2,1,0:T(2,128)(2,1)} %param.16), channel_id=1, source_target_pairs={{0,4},{4,8},{8,12},{1,5},{5,9},{9,13},{2,6},{6,10},{10,14},{3,7},{... | collective-permute-start | bytes 786440 | tf_op jit(solution)/shard_map/ppermute | solution.py:17
  10.9 1.0 reshape.130
  11.9 5.6 %collective-permute-done = bf16[64,2,1024]{2,1,0:T(2,128)(2,1)S(1)} collective-permute-done((bf16[64,2,1024]{2,1,0:T(2,128)(2,1)}, bf16[64,2,1024]{2,1,0:T(2,128)(2,1)S(1)}, u32[]{:S(2)}, u32[]{:S(2)}) %collective-permute-start) | collective-permute-done | bytes 262176 | tf_op jit(solution)/shard_map/ppermute | solution.py:17
  17.5 2.2 fusion.36
  19.8 1.2 reshape.120
  20.9 4.3 %fusion.37 = (f32[128]{0:T(128)S(1)}, bf16[128,1024]{1,0:T(8,128)(2,1)S(1)}) fusion(f32[128,1024]{1,0:T(8,128)S(1)} %reshape.130, bf16[128,3072]{1,0:T(8,128)(2,1)} %reshape.120, bf16[3072,1024]{1,0:T(8,128)(2,1)} %bitcast.105), kind=kOutput, calls=%fused_computation.62 | convolution fusion | flops 806485888 | bytes 7864832 | tf_op jit(solution)/shard_map/dot_general | solution.py:144
  25.3 0.8 fusion.39
  26.2 1.8 copy.29
  27.9 16.1 %all-gather.8.cloned.1.call-done = bf16[512,1024]{1,0:T(8,128)(2,1)} async-done(((bf16[128,1024]{1,0:T(8,128)(2,1)}), bf16[512,1024]{1,0:T(8,128)(2,1)}) %all-gather.8.cloned.1.call-update) | async-done | bytes 1048592 | tf_op jit(solution)/shard_map/all_gather | solution.py:156
  44.1 2.7 %convolution_convert_fusion.1 = bf16[512,768]{1,0:T(8,128)(2,1)S(1)} fusion(bf16[512,1024]{1,0:T(8,128)(2,1)} %all-gather.8.cloned.1.call-done, bf16[1024,768]{0,1:T(8,128)(2,1)} %bitcast.95), kind=kOutput, calls=%fused_computation.53 | convolution fusion | flops 805699584 | bytes 3407872 | tf_op jit(solution)/shard_map/dot_general | solution.py:155
  46.8 0.9 fusion.47
  47.8 0.7 all-gather.12.cloned.1.call-update
  49.5 25.8 %all-gather.10.cloned.1.call-done = bf16[2048,256]{1,0:T(8,128)(2,1)} async-done(((bf16[512,256]{1,0:T(8,128)(2,1)}), bf16[2048,256]{1,0:T(8,128)(2,1)}) %all-gather.10.cloned.1.call-update) | async-done | bytes 1048592 | tf_op jit(solution)/shard_map/all_gather | solution.py:47
  75.3 3.3 %reshape.145 = bf16[4,512,4,64]{3,2,1,0:T(4,128)(2,1)S(1)} reshape(bf16[2048,256]{1,0:T(8,128)(2,1)} %all-gather.10.cloned.1.call-done) | data formatting | bytes 2097152 | tf_op jit(solution)/shard_map/reshape | solution.py:52
  78.6 2.3 %copy.33 = bf16[4,512,4,64]{1,3,2,0:T(8,128)(2,1)} copy(bf16[4,512,4,64]{3,2,1,0:T(4,128)(2,1)S(1)} %reshape.145) | data formatting | bytes 2097152
  81.0 23.4 %all-gather.12.cloned.1.call-done = bf16[2048,256]{1,0:T(8,128)(2,1)} async-done(((bf16[512,256]{1,0:T(8,128)(2,1)}), bf16[2048,256]{1,0:T(8,128)(2,1)}) %all-gather.12.cloned.1.call-update) | async-done | bytes 1048592 | tf_op jit(solution)/shard_map/all_gather | solution.py:48
  104.3 3.3 %reshape.146 = bf16[4,512,4,64]{3,2,1,0:T(4,128)(2,1)S(1)} reshape(bf16[2048,256]{1,0:T(8,128)(2,1)} %all-gather.12.cloned.1.call-done) | data formatting | bytes 2097152 | tf_op jit(solution)/shard_map/reshape | solution.py:53
  107.7 2.4 %copy.34 = bf16[4,512,4,64]{1,3,2,0:T(8,128)(2,1)} copy(bf16[4,512,4,64]{3,2,1,0:T(4,128)(2,1)S(1)} %reshape.146) | data formatting | bytes 2097152
  110.1 24.5 %while.49 = (s32[]{:T(128)}, f32[512,4]{0,1:T(4,128)S(1)}, f32[512,4]{0,1:T(4,128)S(1)}, f32[512,4,64]{0,2,1:T(8,128)S(1)}, s32[4]{0:T(128)S(1)}, /*index=5*/s32...) while((s32[]{:T(128)}, f32[512,4]{0,1:T(4,128)S(1)}, ...), condition=%wide.region_7.8_spmd.clone, body=%wide.region_2.7_spmd.clone.sunk | while | flops 282612256 | bytes 15621669 | solution.py:87
  110.1 0.7 dynamic_slice.96
  112.1 5.5 %conditional.3 = ((f32[512,4]{0,1:T(4,128)S(1)}, f32[512,4]{0,1:T(4,128)S(1)}, f32[512,4,64]{0,2,1:T(8,128)S(1)})) conditional(s32[]{:T(128)} %convert_element_type.108, (f32[512,4]{0,1:T(4,128)S(1)}, f32[512,4]{0,1:T(4,128)S(1)}, f32[512,4,64]{0,2,1:T(8,128)S(1)}) %tuple.127, (s32[]{:T(128)}, s32[]{:T(128)}, bf16[4,512,4,64]{1,3,2,0:T(8,128)(2,1)}, ...), branch_computations={%region_3.3_spmd, %region_4.6_spmd.clone} | conditional | flops 282611712 | bytes 15617068 | solution.py:84
  112.3 1.9 fusion.6
  114.2 1.0 fusion.8
  115.3 2.3 %fusion.15 = f32[512,4,64]{0,2,1:T(8,128)S(1)} fusion(f32[4,512,512]{2,1,0:T(8,128)S(1)} %get-tuple-element.626, f32[512,4]{0,1:T(4,128)S(1)} %max.5, pred[512,512]{0,1:T(8,128)(4,1)S(1)} %broadcast_compare_fusion, f32[512,4,64]{0,2,1:T(8,128)S(1)} %get-tuple-element.540, bf16[4,512,4,64]{1,3,2,0:T(8,128)(2,1)} %get-tuple-element.541, ...), kind=kOutput, calls=%fused_computation.21 | convolution fusion | flops 139722752 | bytes 5784064 | tf_op jit(solution)/shard_map/while/body/eval_jaxpr/cond/branch_1_fun/qhk,khd->qhd/dot_general | solution.py:75
  119.6 5.5 %conditional.3 = ((f32[512,4]{0,1:T(4,128)S(1)}, f32[512,4]{0,1:T(4,128)S(1)}, f32[512,4,64]{0,2,1:T(8,128)S(1)})) conditional(s32[]{:T(128)} %convert_element_type.108, (f32[512,4]{0,1:T(4,128)S(1)}, f32[512,4]{0,1:T(4,128)S(1)}, f32[512,4,64]{0,2,1:T(8,128)S(1)}) %tuple.127, (s32[]{:T(128)}, s32[]{:T(128)}, bf16[4,512,4,64]{1,3,2,0:T(8,128)(2,1)}, ...), branch_computations={%region_3.3_spmd, %region_4.6_spmd.clone} | conditional | flops 282611712 | bytes 15617068 | solution.py:84
  119.9 1.9 fusion.6
  121.7 1.0 fusion.8
  122.8 2.3 %fusion.15 = f32[512,4,64]{0,2,1:T(8,128)S(1)} fusion(f32[4,512,512]{2,1,0:T(8,128)S(1)} %get-tuple-element.626, f32[512,4]{0,1:T(4,128)S(1)} %max.5, pred[512,512]{0,1:T(8,128)(4,1)S(1)} %broadcast_compare_fusion, f32[512,4,64]{0,2,1:T(8,128)S(1)} %get-tuple-element.540, bf16[4,512,4,64]{1,3,2,0:T(8,128)(2,1)} %get-tuple-element.541, ...), kind=kOutput, calls=%fused_computation.21 | convolution fusion | flops 139722752 | bytes 5784064 | tf_op jit(solution)/shard_map/while/body/eval_jaxpr/cond/branch_1_fun/qhk,khd->qhd/dot_general | solution.py:75
  127.1 5.5 %conditional.3 = ((f32[512,4]{0,1:T(4,128)S(1)}, f32[512,4]{0,1:T(4,128)S(1)}, f32[512,4,64]{0,2,1:T(8,128)S(1)})) conditional(s32[]{:T(128)} %convert_element_type.108, (f32[512,4]{0,1:T(4,128)S(1)}, f32[512,4]{0,1:T(4,128)S(1)}, f32[512,4,64]{0,2,1:T(8,128)S(1)}) %tuple.127, (s32[]{:T(128)}, s32[]{:T(128)}, bf16[4,512,4,64]{1,3,2,0:T(8,128)(2,1)}, ...), branch_computations={%region_3.3_spmd, %region_4.6_spmd.clone} | conditional | flops 282611712 | bytes 15617068 | solution.py:84
  127.4 1.9 fusion.6
  129.2 1.0 fusion.8
  130.3 2.3 %fusion.15 = f32[512,4,64]{0,2,1:T(8,128)S(1)} fusion(f32[4,512,512]{2,1,0:T(8,128)S(1)} %get-tuple-element.626, f32[512,4]{0,1:T(4,128)S(1)} %max.5, pred[512,512]{0,1:T(8,128)(4,1)S(1)} %broadcast_compare_fusion, f32[512,4,64]{0,2,1:T(8,128)S(1)} %get-tuple-element.540, bf16[4,512,4,64]{1,3,2,0:T(8,128)(2,1)} %get-tuple-element.541, ...), kind=kOutput, calls=%fused_computation.21 | convolution fusion | flops 139722752 | bytes 5784064 | tf_op jit(solution)/shard_map/while/body/eval_jaxpr/cond/branch_1_fun/qhk,khd->qhd/dot_general | solution.py:75
  134.8 1.4 convolution_convert_fusion
  137.2 29.5 %reduce-scatter.2.cloned.1.call-done = bf16[128,1024]{1,0:T(8,128)(2,1)} async-done(((bf16[512,1024]{1,0:T(8,128)(2,1)}), bf16[128,1024]{1,0:T(8,128)(2,1)}) %reduce-scatter.2.cloned.1.call-update) | async-done | bytes 262160 | tf_op jit(solution)/shard_map/reduce_scatter | solution.py:170
  166.8 1.0 fusion.40
  168.0 5.2 %all_gather.27 = bf16[16,512]{1,0:T(8,128)(2,1)S(1)} all-gather(bf16[16,128]{1,0:T(8,128)(2,1)S(1)} %fusion.34), channel_id=1, replica_groups=mesh['groups'=2,'frames'=4,'code'=2,'head'=2] {'code','head'}, dimensions={1}, use_global_device_ids=true | all-gather | bytes 20480 | tf_op jit(solution)/shard_map/all_gather | solution.py:183
  173.2 37.9 %while.50 = (s32[]{:T(128)}, f32[512]{0:T(512)S(1)}, f32[512]{0:T(512)S(1)}, f32[512]{0:T(512)S(1)}, bf16[4,16,4096]{2,1,0:T(8,128)(2,1)S(1)}, /*index=5*/bf16[1...) while((s32[]{:T(128)}, f32[512]{0:T(512)S(1)}, ...), condition=%wide.wide.region_14.15_spmd.clone, body=%wide.wide.region_10.14_spmd.clone.sunk | while | flops 84083712 | bytes 17141940 | solution.py:122
  173.2 4.2 %fusion.65 = (f32[512]{0:T(512)S(1)}, f32[4096,512]{1,0:T(8,128)}) fusion(f32[4096]{0:T(1024)S(1)} %multiply_reduce_fusion.4, bf16[16,512]{1,0:T(8,128)(2,1)S(1)} %get-tuple-element.931, bf16[4,16,4096]{2,1,0:T(8,128)(2,1)S(1)} %get-tuple-element.930, s32[]{:T(128)} %get-tuple-element.913, f32[512]{0:T(512)S(1)} %get-tuple-element.929), kind=kOutput, calls=%fused_computation.80.clone.clone.1 | convolution fusion | flops 77594112 | bytes 8556548 | tf_op jit(solution)/shard_map/while/body/eval_jaxpr/dot_general | solution.py:111
  178.7 4.0 %fusion.66 = f32[512]{0:T(512)S(1)} fusion(f32[4096,512]{1,0:T(8,128)} %get-tuple-element.839, s32[512]{0:T(512)S(1)} %get-tuple-element.935, s32[4096]{0:T(1024)S(1)} %iota_add_fusion.4), kind=kLoop, calls=%fused_computation.4.clone.clone.1 | loop fusion | flops 6290944 | bytes 8409088 | tf_op jit(solution)/shard_map/while/body/eval_jaxpr/reduce_sum | solution.py:117
  182.7 4.2 %fusion.65 = (f32[512]{0:T(512)S(1)}, f32[4096,512]{1,0:T(8,128)}) fusion(f32[4096]{0:T(1024)S(1)} %multiply_reduce_fusion.4, bf16[16,512]{1,0:T(8,128)(2,1)S(1)} %get-tuple-element.931, bf16[4,16,4096]{2,1,0:T(8,128)(2,1)S(1)} %get-tuple-element.930, s32[]{:T(128)} %get-tuple-element.913, f32[512]{0:T(512)S(1)} %get-tuple-element.929), kind=kOutput, calls=%fused_computation.80.clone.clone.1 | convolution fusion | flops 77594112 | bytes 8556548 | tf_op jit(solution)/shard_map/while/body/eval_jaxpr/dot_general | solution.py:111
  188.1 4.0 %fusion.66 = f32[512]{0:T(512)S(1)} fusion(f32[4096,512]{1,0:T(8,128)} %get-tuple-element.839, s32[512]{0:T(512)S(1)} %get-tuple-element.935, s32[4096]{0:T(1024)S(1)} %iota_add_fusion.4), kind=kLoop, calls=%fused_computation.4.clone.clone.1 | loop fusion | flops 6290944 | bytes 8409088 | tf_op jit(solution)/shard_map/while/body/eval_jaxpr/reduce_sum | solution.py:117
  192.2 4.2 %fusion.65 = (f32[512]{0:T(512)S(1)}, f32[4096,512]{1,0:T(8,128)}) fusion(f32[4096]{0:T(1024)S(1)} %multiply_reduce_fusion.4, bf16[16,512]{1,0:T(8,128)(2,1)S(1)} %get-tuple-element.931, bf16[4,16,4096]{2,1,0:T(8,128)(2,1)S(1)} %get-tuple-element.930, s32[]{:T(128)} %get-tuple-element.913, f32[512]{0:T(512)S(1)} %get-tuple-element.929), kind=kOutput, calls=%fused_computation.80.clone.clone.1 | convolution fusion | flops 77594112 | bytes 8556548 | tf_op jit(solution)/shard_map/while/body/eval_jaxpr/dot_general | solution.py:111
  197.6 4.0 %fusion.66 = f32[512]{0:T(512)S(1)} fusion(f32[4096,512]{1,0:T(8,128)} %get-tuple-element.839, s32[512]{0:T(512)S(1)} %get-tuple-element.935, s32[4096]{0:T(1024)S(1)} %iota_add_fusion.4), kind=kLoop, calls=%fused_computation.4.clone.clone.1 | loop fusion | flops 6290944 | bytes 8409088 | tf_op jit(solution)/shard_map/while/body/eval_jaxpr/reduce_sum | solution.py:117
  201.7 4.2 %fusion.65 = (f32[512]{0:T(512)S(1)}, f32[4096,512]{1,0:T(8,128)}) fusion(f32[4096]{0:T(1024)S(1)} %multiply_reduce_fusion.4, bf16[16,512]{1,0:T(8,128)(2,1)S(1)} %get-tuple-element.931, bf16[4,16,4096]{2,1,0:T(8,128)(2,1)S(1)} %get-tuple-element.930, s32[]{:T(128)} %get-tuple-element.913, f32[512]{0:T(512)S(1)} %get-tuple-element.929), kind=kOutput, calls=%fused_computation.80.clone.clone.1 | convolution fusion | flops 77594112 | bytes 8556548 | tf_op jit(solution)/shard_map/while/body/eval_jaxpr/dot_general | solution.py:111
  207.1 4.0 %fusion.66 = f32[512]{0:T(512)S(1)} fusion(f32[4096,512]{1,0:T(8,128)} %get-tuple-element.839, s32[512]{0:T(512)S(1)} %get-tuple-element.935, s32[4096]{0:T(1024)S(1)} %iota_add_fusion.4), kind=kLoop, calls=%fused_computation.4.clone.clone.1 | loop fusion | flops 6290944 | bytes 8409088 | tf_op jit(solution)/shard_map/while/body/eval_jaxpr/reduce_sum | solution.py:117
  211.1 5.2 %all-gather.2 = f32[4,1,512]{2,1,0:T(1,128)S(1)} all-gather(f32[1,1,512]{2,1,0:T(1,128)S(1)} %bitcast.101), channel_id=2, replica_groups=mesh['groups'=2,'frames'=4,'code'=2,'head'=2] {'code','head'}, dimensions={0}, use_global_device_ids=true | all-gather | bytes 10240 | tf_op jit(solution)/shard_map/all_gather | solution.py:21
  216.3 5.1 %all-gather.3 = f32[4,1,512]{2,1,0:T(1,128)S(1)} all-gather(f32[1,1,512]{2,1,0:T(1,128)S(1)} %bitcast.102), channel_id=3, replica_groups=mesh['groups'=2,'frames'=4,'code'=2,'head'=2] {'code','head'}, dimensions={0}, use_global_device_ids=true | all-gather | bytes 10240 | tf_op jit(solution)/shard_map/all_gather | solution.py:21
  221.4 0.8 reshape.126
  (104 shorter events, 9.8 us)
Async XLA Ops:
  7.2 127.6 %copy-start = (bf16[256,1024]{1,0:T(8,128)(2,1)S(1)}, bf16[256,1024]{1,0:T(8,128)(2,1)}, u32[]{:S(2)}) copy-start(bf16[256,1024]{1,0:T(8,128)(2,1)} %param.20) | copy-start | bytes 1572868
  7.2 36.9 %all-gather.8.cloned.1.call-start = ((), (), s32[]{:S(2)}) async-start(), calls=%async_computation.1 | async-start | bytes 1310720 | tf_op jit(solution)/shard_map/all_gather | solution.py:156
  7.2 10.3 %collective-permute-start = (bf16[64,2,1024]{2,1,0:T(2,128)(2,1)}, bf16[64,2,1024]{2,1,0:T(2,128)(2,1)S(1)}, u32[]{:S(2)}, u32[]{:S(2)}) collective-permute-start(bf16[64,2,1024]{2,1,0:T(2,128)(2,1)} %param.16), channel_id=1, source_target_pairs={{0,4},{4,8},{8,12},{1,5},{5,9},{9,13},{2,6},{6,10},{10,14},{3,7},{... | collective-permute-start | bytes 786440 | tf_op jit(solution)/shard_map/ppermute | solution.py:17
  20.9 4.3 %copy-start.7 = (f32[1024]{0:T(1024)S(1)}, f32[1024]{0:T(1024)}, u32[]{:S(2)}) copy-start(f32[1024]{0:T(1024)} %param.18) | copy-start | bytes 12292
  20.9 5.2 %copy-start.1 = (bf16[1024,3,256]{2,0,1:T(8,128)(2,1)S(1)}, bf16[1024,3,256]{2,0,1:T(8,128)(2,1)}, u32[]{:S(2)}) copy-start(bf16[1024,3,256]{2,0,1:T(8,128)(2,1)} %param.19) | copy-start | bytes 4718596
  25.2 21.6 %copy-start.2 = (bf16[128,1024]{1,0:T(8,128)(2,1)}, bf16[128,1024]{1,0:T(8,128)(2,1)S(1)}, u32[]{:S(2)}) copy-start(bf16[128,1024]{1,0:T(8,128)(2,1)S(1)} %get-tuple-element.618) | copy-start | bytes 786436
  26.1 49.2 %all-gather.10.cloned.1.call-start = ((), (), s32[]{:S(2)}) async-start(), calls=%async_computation.2 | async-start | bytes 1310720 | tf_op jit(solution)/shard_map/all_gather | solution.py:47
  47.7 56.6 %all-gather.12.cloned.1.call-start = ((), (), s32[]{:S(2)}) async-start(), calls=%async_computation.3 | async-start | bytes 1310720 | tf_op jit(solution)/shard_map/all_gather | solution.py:48
  48.4 118.3 %reduce-scatter.2.cloned.1.call-start = ((), (), s32[]{:S(2)}) async-start(), calls=%async_computation.4 | async-start | bytes 1310720 | tf_op jit(solution)/shard_map/reduce_scatter | solution.py:170
  110.1 26.1 %copy-start.8 = (s32[256,2]{0,1:T(2,128)S(1)}, s32[256,2]{0,1:T(2,128)}, u32[]{:S(2)}) copy-start(s32[256,2]{0,1:T(2,128)} %param.23) | copy-start | bytes 6148
  134.6 1.9 copy-start.4
  134.7 32.1 %copy-start.3 = (bf16[128,1024]{1,0:T(8,128)(2,1)S(1)}, bf16[128,1024]{1,0:T(8,128)(2,1)}, u32[]{:S(2)}) copy-start(bf16[128,1024]{1,0:T(8,128)(2,1)} %copy-done.2) | copy-start | bytes 786436
  134.7 33.1 %copy-start.6 = (bf16[1024,16]{0,1:T(8,128)(2,1)S(1)}, bf16[1024,16]{0,1:T(8,128)(2,1)}, u32[]{:S(2)}) copy-start(bf16[1024,16]{0,1:T(8,128)(2,1)} %param.21) | copy-start | bytes 98308
  136.4 36.8 %copy-start.5 = (s32[256,2]{1,0:T(8,128)}, s32[256,2]{1,0:T(8,128)S(1)}, u32[]{:S(2)}) copy-start(s32[256,2]{1,0:T(8,128)S(1)} %copy.36) | copy-start | bytes 6148
Sparse Core Ops, SparseCore 0:
  26.2 17.7 all-gather.7
  47.8 27.4 all-gather.9
  76.9 27.4 all-gather.11
  136.3 30.3 reduce-scatter.1
where the time goes:
time: 233 us; the launch traced here: 231 us
  waiting for transfers between devices  101 us (43%)
  matrix products  37.8 us (16%)
  other arithmetic  25 us (11%)
  local copies, waits for them, and re-layouts  24.7 us (11%)
  blocking collectives  15.5 us (7%)
  between operations  14.1 us (6%)
  loops' own time  8.35 us (4%)
  starting transfers between devices  3.96 us (2%)
    reduce_scatter x1, waiting for transfers between devices, shards(): lax.psum_scatter(jnp.dot(attended, out_weight, preferred_element_type=jnp...  29.5 us
    all_gather x1, waiting for transfers between devices, attend_slab(): key_part = lax.all_gather(keys, 'frames', axis=0, tiled=True)  25.8 us
    all_gather x1, waiting for transfers between devices, attend_slab(): value_part = lax.all_gather(values, 'frames', axis=0, tiled=True)  23.4 us
    dot_general x4, matrix products, scan_visit(): lax.dot_general(latent_t, code_block, (((0,), (0,)), ((), ())), preferred...  16.6 us
    all_gather x1, waiting for transfers between devices, shards(): lax.all_gather(normed, ('code', 'head'), axis=0, tiled=True)  16.1 us
    reduce_sum x4, other arithmetic, scan_visit(): jnp.sum(jnp.where(labels[None, :] == wanted[:, None], distance, 0.0), axi...  15.9 us
    all_gather x2, blocking collectives, merged(): everything = jax.tree.map(lambda part: lax.all_gather(part, axis), value)  10.3 us
    unnamed x27, local copies, waits for them, and re-layouts  8.2 us
  transfers between devices with their start and end apart: 5, of which 5 were waited for; matrix products, arithmetic and copies ran while one was open for 4% of the time, Pallas kernels for 0%

commit v1 on v0

v1 whole, which is shorter than its diff:
```python
import functools
import math

import jax
import jax.numpy as jnp
from jax import lax
from jax.experimental import pallas as pl
from jax.experimental.pallas import tpu as pltpu
from jax.sharding import PartitionSpec as P

HEADS = 16
EPSILON = 1e-06
LANES = 128
MESH = pl.DeviceIdType.MESH
BF16 = jnp.bfloat16
F32 = jnp.float32


def tile_of(length, most):
    return math.gcd(length, most)


def encoder_kernel(
    n_f, n_c, n_h,
    video_ref, conv_w_hbm, gain_ref, qkv_w_hbm, out_w_hbm, latent_w_ref, codes_hbm, wanted_ref,
    encoded_ref, least_ref, gap_ref,
    ext, conv_w, mixed, block_input, normed, qkv_w, queries, kv, top, denom, summed,
    attended, gathered, out_w, codes, augmented, lhs, wanted,
    local_sems, send_sems, recv_sems, kv_send, kv_recv, halo_send, halo_recv,
):
    n_g = n_c * n_h
    fr = lax.axis_index("frames")
    c = lax.axis_index("code")
    h = lax.axis_index("head")
    g = c * n_h + h
    fh, pos, width = video_ref.shape
    rows = fh * pos
    chip_rows = n_h * rows
    lw = out_w_hbm.shape[0]
    pairs = lw // LANES
    head_dim = width // HEADS
    per_tile = LANES // head_dim
    slab = n_g * rows
    code_dim, shard = codes_hbm.shape

    def device(c2, h2):
        return {"code": c2, "head": h2}

    conv_copies = [
        pltpu.make_async_copy(conv_w_hbm.at[k], conv_w.at[k], local_sems.at[k]) for k in range(3)
    ]
    qkv_copy = pltpu.make_async_copy(qkv_w_hbm, qkv_w, local_sems.at[3])
    out_copy = pltpu.make_async_copy(out_w_hbm, out_w.at[g], local_sems.at[4])
    codes_copy = pltpu.make_async_copy(codes_hbm, codes.at[g], local_sems.at[5])
    for copy in [codes_copy] + conv_copies + [qkv_copy, out_copy]:
        copy.start()

    barrier = pltpu.get_barrier_semaphore()
    for dc in range(n_c):
        for dh in range(n_h):
            if dc or dh:
                pl.semaphore_signal(
                    barrier, inc=1,
                    device_id=device(lax.rem(c + dc, n_c), lax.rem(h + dh, n_h)),
                    device_id_type=MESH,
                )
    for df in range(1, n_f):
        pl.semaphore_signal(
            barrier, inc=1, device_id={"frames": lax.rem(fr + df, n_f)}, device_id_type=MESH
        )
    pl.semaphore_wait(barrier, n_g - 1 + n_f - 1)

    halo = pltpu.make_async_remote_copy(
        src_ref=video_ref.at[pl.ds(fh - 2, 2)],
        dst_ref=ext.at[pl.ds(0, 2)],
        send_sem=halo_send,
        recv_sem=halo_recv,
        device_id={"frames": lax.rem(fr + 1, n_f)},
        device_id_type=MESH,
    )

    @pl.when(fr + 1 < n_f)
    def _():
        halo.start()

    started = []

    def send(kind, block, slot, c2, h2):
        copy = pltpu.make_async_remote_copy(
            src_ref=block(slot),
            dst_ref=block(slot),
            send_sem=send_sems.at[len(started)],
            recv_sem=recv_sems.at[kind, slot],
            device_id=device(c2, h2),
            device_id_type=MESH,
        )
        copy.start()
        started.append(copy)

    def arrived(kind, block, slot):
        pltpu.make_async_remote_copy(
            src_ref=block(slot),
            dst_ref=block(slot),
            send_sem=send_sems.at[0],
            recv_sem=recv_sems.at[kind, slot],
            device_id=device(c, lax.rem(h + 1, n_h)),
            device_id_type=MESH,
        ).wait_recv()

    def slot_of(dc, dh):
        return lax.rem(c + n_c - dc, n_c) * n_h + lax.rem(h + n_h - dh, n_h)

    def spread(kind, block):
        for dc in range(1, n_c):
            send(kind, block, g, lax.rem(c + dc, n_c), h)
        for dh in range(1, n_h):
            send(kind, block, g, c, lax.rem(h + dh, n_h))

    def forward(kind, block, dc):
        slot = slot_of(dc, 0)
        arrived(kind, block, slot)
        for dh in range(1, n_h):
            send(kind, block, slot, c, lax.rem(h + dh, n_h))

    def rest(kind, block, dc):
        for dh in range(1, n_h):
            arrived(kind, block, slot_of(dc, dh))

    def codes_block(slot):
        return codes.at[slot]

    def normed_block(slot):
        return normed.at[pl.ds(pl.multiple_of(slot * rows, rows), rows)]

    def out_block(slot):
        return out_w.at[slot]

    codes_copy.wait()
    spread(0, codes_block)

    ext[2:] = video_ref[...]
    tile = tile_of(width, 256)

    def tap(k):
        conv_copies[k].wait()
        taken = ext[2 - k : 2 - k + fh].reshape(rows, width)

        @pl.loop(0, width // tile)
        def _(n):
            cols = pl.ds(pl.multiple_of(n * tile, tile), tile)
            part = jnp.dot(taken, conv_w[k, :, cols], preferred_element_type=F32)
            if k == 0:
                mixed[:, cols] = part
            else:
                mixed[:, cols] = mixed[:, cols] + part

    tap(0)

    @pl.when(fr > 0)
    def _():
        halo.wait_recv()

    @pl.when(fr == 0)
    def _():
        ext[:2] = jnp.zeros((2, pos, width), BF16)

    tap(1)
    tap(2)
    conv = mixed[...]
    values = (video_ref[...].reshape(rows, width).astype(F32) + conv / (1.0 + jnp.exp(-conv))).astype(BF16)
    block_input[...] = values
    values32 = values.astype(F32)
    mean_square = jnp.mean(values32 * values32, axis=-1, keepdims=True)
    normed[pl.ds(pl.multiple_of(g * rows, rows), rows), :] = (
        values32 * lax.rsqrt(mean_square + EPSILON) * gain_ref[...]
    ).astype(BF16)
    spread(1, normed_block)

    def project(c2):
        at = pl.ds(pl.multiple_of(c2 * chip_rows, chip_rows), chip_rows)
        taken = normed[at, :]
        for kind in range(3):
            out = jnp.dot(taken, qkv_w[kind], preferred_element_type=F32)
            out = out.astype(BF16)
            for p in range(pairs):
                piece = out[:, p * LANES : (p + 1) * LANES]
                if kind == 0:
                    queries[p, at, :] = piece * (1.0 / math.sqrt(head_dim))
                else:
                    kv[fr, kind - 1, p, at, :] = piece

    qkv_copy.wait()
    rest(1, normed_block, 0)
    project(c)
    for dc in range(1, n_c):
        forward(1, normed_block, dc)
    out_copy.wait()
    spread(2, out_block)
    for dc in range(1, n_c):
        rest(1, normed_block, dc)
        project(lax.rem(c + n_c - dc, n_c))

    def kv_copy(slot, df):
        return pltpu.make_async_remote_copy(
            src_ref=kv.at[slot],
            dst_ref=kv.at[slot],
            send_sem=kv_send.at[df],
            recv_sem=kv_recv.at[slot],
            device_id={"frames": lax.rem(fr + df, n_f)},
            device_id_type=MESH,
        )

    for df in range(1, n_f):
        @pl.when(fr + df < n_f)
        def _():
            kv_copy(fr, df).start()

    q_tile = tile_of(slab, 256)
    lane = lax.broadcasted_iota(jnp.int32, (q_tile, LANES), 1) // head_dim

    def by_head(parts):
        out = parts[0]
        for k in range(1, per_tile):
            out = jnp.where(lane == k, parts[k], out)
        return out

    def absorb(slot, own):
        @pl.loop(0, pairs * (slab // q_tile))
        def _(step):
            p = step // (slab // q_tile)
            first = (step % (slab // q_tile)) * q_tile
            at = pl.ds(pl.multiple_of(first, q_tile), q_tile)
            q = queries[p, at, :]
            k = kv[slot, 0, p]
            v = kv[slot, 1, p]
            if own:
                q_row = first + lax.broadcasted_iota(jnp.int32, (q_tile, slab), 0)
                k_row = lax.broadcasted_iota(jnp.int32, (q_tile, slab), 1)
                allowed = (k_row // pos) % fh <= (q_row // pos) % fh
            else:
                old_top = top[p, at, :]
            tops, factors, sums, outs = [], [], [], []
            for hh in range(per_tile):
                mine = jnp.where(lane == hh, q, jnp.zeros_like(q))
                scores = lax.dot_general(mine, k, (((1,), (1,)), ((), ())), preferred_element_type=F32)
                if own:
                    scores = jnp.where(allowed, scores, -1e30)
                fresh = jnp.max(scores, axis=1, keepdims=True)
                if not own:
                    old = old_top[:, hh * head_dim : hh * head_dim + 1]
                    fresh = jnp.maximum(fresh, old)
                    factors.append(jnp.exp(old - fresh))
                weights = jnp.exp(scores - fresh)
                tops.append(fresh)
                sums.append(jnp.sum(weights, axis=1, keepdims=True))
                outs.append(jnp.dot(weights.astype(BF16), v, preferred_element_type=F32))
            top[p, at, :] = by_head([jnp.broadcast_to(x, (q_tile, LANES)) for x in tops])
            total = by_head([jnp.broadcast_to(x, (q_tile, LANES)) for x in sums])
            out = by_head(outs)
            if own:
                denom[p, at, :] = total
                summed[p, at, :] = out
            else:
                factor = by_head([jnp.broadcast_to(x, (q_tile, LANES)) for x in factors])
                denom[p, at, :] = denom[p, at, :] * factor + total
                summed[p, at, :] = summed[p, at, :] * factor + out

    absorb(fr, True)

    for dc in range(1, n_c):
        forward(0, codes_block, dc)
    for dc in range(n_c):
        rest(0, codes_block, dc)
    c_tile = tile_of(shard, 1024)

    @pl.loop(0, n_g * (shard // c_tile))
    def _(step):
        slot = step // (shard // c_tile)
        cols = pl.ds(pl.multiple_of((step % (shard // c_tile)) * c_tile, c_tile), c_tile)
        block = codes[slot, :, cols]
        block32 = block.astype(F32)
        squares = jnp.sum(block32 * block32, axis=0, keepdims=True)
        high = squares.astype(BF16).astype(F32)
        middle = (squares - high).astype(BF16).astype(F32)
        low = squares - high - middle
        row = lax.broadcasted_iota(jnp.int32, (code_dim, c_tile), 0)
        extra = jnp.where(row == 0, high, jnp.where(row == 1, middle, jnp.where(row == 2, low, 0.0)))
        augmented[slot, :code_dim, cols] = block
        augmented[slot, code_dim:, cols] = extra.astype(BF16)

    for dc in range(1, n_c):
        forward(2, out_block, dc)
    for dc in range(n_c):
        rest(2, out_block, dc)

    def visit(k, carry):
        slot = fr - 1 - k
        kv_copy(slot, 1).wait_recv()
        absorb(slot, False)
        return carry

    lax.fori_loop(0, fr, visit, 0)

    for p in range(pairs):
        attended[:, p * LANES : (p + 1) * LANES] = (summed[p] / denom[p]).astype(BF16)

    def rows_at(slot):
        return pl.ds(pl.multiple_of(slot * rows, rows), rows)

    def exchange(dc, dh):
        c2, h2 = lax.rem(c + dc, n_c), lax.rem(h + dh, n_h)
        copy = pltpu.make_async_remote_copy(
            src_ref=attended.at[rows_at(c2 * n_h + h2)],
            dst_ref=gathered.at[g],
            send_sem=send_sems.at[len(started)],
            recv_sem=recv_sems.at[3, g],
            device_id=device(c2, h2),
            device_id_type=MESH,
        )
        copy.start()
        started.append(copy)

    order = [(dc, dh) for dc in range(n_c) for dh in range(n_h) if dc or dh]
    for dc, dh in reversed(order):
        exchange(dc, dh)

    def project_out(taken, slot, fresh):
        @pl.loop(0, width // tile)
        def _(n):
            cols = pl.ds(pl.multiple_of(n * tile, tile), tile)
            part = jnp.dot(taken, out_w[slot, :, cols], preferred_element_type=F32)
            if fresh:
                mixed[:, cols] = part
            else:
                mixed[:, cols] = mixed[:, cols] + part

    project_out(attended[rows_at(g), :], g, True)
    for dc, dh in order:
        slot = slot_of(dc, dh)
        arrived(3, lambda s: gathered.at[s], slot)
        project_out(gathered[slot], slot, False)

    encoded = (block_input[...].astype(F32) + mixed[...]).astype(BF16)
    encoded_ref[...] = encoded.reshape(fh, pos, width)
    latent = lax.dot_general(
        encoded, latent_w_ref[...], (((1,), (1,)), ((), ())), preferred_element_type=F32
    ).astype(BF16).astype(F32)
    square = jnp.sum(latent * latent, axis=1, keepdims=True)
    column = lax.broadcasted_iota(jnp.int32, lhs.shape, 1)
    lhs[...] = jnp.where(column < code_dim + 3, 1.0, 0.0)
    lhs[:, :code_dim] = -2.0 * latent
    left = lhs[...].astype(BF16)

    everyone = (pos, wanted_ref.shape[1])
    is_mine = lax.broadcasted_iota(jnp.int32, everyone, 0) + g * pos == lax.broadcasted_iota(
        jnp.int32, everyone, 1
    )
    for t in range(fh):
        mine = jnp.where(is_mine, jnp.broadcast_to(wanted_ref[t : t + 1, :], everyone), 0)
        wanted[t * pos : (t + 1) * pos, :] = jnp.broadcast_to(
            jnp.sum(mine, axis=1, keepdims=True), (pos, LANES)
        )
    lanes = lax.broadcasted_iota(jnp.int32, (1, LANES), 1)

    def search(step, state):
        least, chosen = state
        slot = step // (shard // c_tile)
        cols = pl.ds(pl.multiple_of((step % (shard // c_tile)) * c_tile, c_tile), c_tile)
        found = jnp.dot(left, augmented[slot, :, cols], preferred_element_type=F32)
        sought = wanted[...]
        for k in range(c_tile // LANES):
            part = found[:, k * LANES : (k + 1) * LANES]
            labels = lanes + (step * c_tile + k * LANES)
            least = jnp.minimum(least, part)
            chosen = jnp.where(sought == labels, part, chosen)
        return least, chosen

    least, chosen = lax.fori_loop(
        0, n_g * (shard // c_tile), search,
        (jnp.full((rows, LANES), 3e38, F32), jnp.zeros((rows, LANES), F32)),
    )
    least = (jnp.min(least, axis=1, keepdims=True) + square) / code_dim
    chosen = (jnp.sum(chosen, axis=1, keepdims=True) + square) / code_dim
    gap = chosen - least
    diagonal = lax.broadcasted_iota(jnp.int32, (pos, pos), 0) == lax.broadcasted_iota(
        jnp.int32, (pos, pos), 1
    )
    for t in range(fh):
        for ref, column in ((least_ref, least), (gap_ref, gap)):
            square_part = jnp.broadcast_to(column[t * pos : (t + 1) * pos], (pos, pos))
            ref[t : t + 1, :] = jnp.sum(
                jnp.where(diagonal, square_part, 0.0), axis=0, keepdims=True
            )

    for copy in started:
        copy.wait_send()

    @pl.when(fr + 1 < n_f)
    def _():
        halo.wait_send()

    for df in range(1, n_f):
        @pl.when(fr + df < n_f)
        def _():
            kv_copy(fr, df).wait_send()


def shards(
    n_f, n_c, n_h,
    video, conv_weight, norm_gain, qkv_weight, out_weight, latent_weight, codebook, reference_codes,
):
    positions, frames_here, width = video.shape
    rows = positions * frames_here
    n_g = n_c * n_h
    slab = n_g * rows
    lw = qkv_weight.shape[2]
    pairs = lw // LANES
    code_dim, shard = codebook.shape
    sends = 3 * (n_c - 1 + n_h - 1 + (n_c - 1) * (n_h - 1)) + n_g - 1
    vmem = pl.BlockSpec(memory_space=pltpu.VMEM)
    anywhere = pl.BlockSpec(memory_space=pl.ANY)
    encoded, least, gap = pl.pallas_call(
        functools.partial(encoder_kernel, n_f, n_c, n_h),
        out_shape=(
            jax.ShapeDtypeStruct((frames_here, positions, width), BF16),
            jax.ShapeDtypeStruct((frames_here, positions), F32),
            jax.ShapeDtypeStruct((frames_here, positions), F32),
        ),
        in_specs=[vmem, anywhere, vmem, anywhere, anywhere, vmem, anywhere, vmem],
        out_specs=(vmem, vmem, vmem),
        scratch_shapes=[
            pltpu.VMEM((2 + frames_here, positions, width), BF16),
            pltpu.VMEM(conv_weight.shape, BF16),
            pltpu.VMEM((rows, width), F32),
            pltpu.VMEM((rows, width), BF16),
            pltpu.VMEM((slab, width), BF16),
            pltpu.VMEM((3, width, lw), BF16),
            pltpu.VMEM((pairs, slab, LANES), BF16),
            pltpu.VMEM((n_f, 2, pairs, slab, LANES), BF16),
            pltpu.VMEM((pairs, slab, LANES), F32),
            pltpu.VMEM((pairs, slab, LANES), F32),
            pltpu.VMEM((pairs, slab, LANES), F32),
            pltpu.VMEM((slab, lw), BF16),
            pltpu.VMEM((n_g, rows, lw), BF16),
            pltpu.VMEM((n_g, lw, width), BF16),
            pltpu.VMEM((n_g, code_dim, shard), BF16),
            pltpu.VMEM((n_g, 2 * code_dim, shard), BF16),
            pltpu.VMEM((rows, 2 * code_dim), F32),
            pltpu.VMEM((rows, LANES), jnp.int32),
            pltpu.SemaphoreType.DMA((6,)),
            pltpu.SemaphoreType.DMA((sends,)),
            pltpu.SemaphoreType.DMA((4, n_g)),
            pltpu.SemaphoreType.DMA((n_f,)),
            pltpu.SemaphoreType.DMA((n_f,)),
            pltpu.SemaphoreType.DMA,
            pltpu.SemaphoreType.DMA,
        ],
        compiler_params=pltpu.CompilerParams(
            collective_id=0, has_side_effects=True, vmem_limit_bytes=48 * 1024 * 1024
        ),
    )(
        jnp.transpose(video, (1, 0, 2)),
        conv_weight,
        norm_gain.reshape(1, width),
        jnp.transpose(qkv_weight, (1, 0, 2)),
        out_weight,
        jnp.transpose(latent_weight),
        codebook,
        jnp.transpose(reference_codes),
    )
    return jnp.transpose(encoded, (1, 0, 2)), jnp.transpose(least), jnp.transpose(gap)


def solution(mesh):
    sizes = [mesh.shape[axis] for axis in ("frames", "code", "head")]
    return jax.shard_map(
        functools.partial(shards, *sizes),
        mesh=mesh,
        in_specs=(
            P(("code", "head"), ("groups", "frames"), None),
            P(),
            P(),
            P(None, None, ("code", "head")),
            P(("code", "head"), None),
            P(),
            P(None, ("code", "head")),
            P(None, ("groups", "frames")),
        ),
        out_specs=(
            P(("code", "head"), ("groups", "frames"), None),
            P(("code", "head"), ("groups", "frames")),
            P(("code", "head"), ("groups", "frames")),
        ),
        check_vma=False,
    )
```

time: 233 us -> 107 us (0.46)
  the two profiles are of different devices: /device:TPU:16 before, /device:TPU:31 now
where the time goes in v1:
time: 107 us
  Pallas kernels  97.3 us (91%)
  local copies, waits for them, and re-layouts  8.7 us (8%)
    pallas_call x1, Pallas kernels, shards(): pl.pallas_call(functools.partial(encoder_kernel, n_f, n_c, n_h), out_shap...  97.3 us
    unnamed x16, local copies, waits for them, and re-layouts  8.7 us

profile of v1, /device:TPU:31, one launch (start us, length us, event | category | flops | bytes accessed | tf_op | source)
XLA Modules:
  0.0 106.7 jit_solution(5137952030916187456)
XLA Ops:
  0.6 1.0 copy.14
  1.6 0.0 copy-start
  1.6 1.4 %copy-done = bf16[1024,3,256]{2,0,1:T(8,128)(2,1)S(1)} copy-done((bf16[1024,3,256]{2,0,1:T(8,128)(2,1)S(1)}, bf16[1024,3,256]{2,0,1:T(8,128)(2,1)}, u32[]{:S(2)}) %copy-start) | copy-done | bytes 1572888
  3.0 0.0 copy-start.1
  3.0 1.0 copy-done.1
  4.1 0.0 copy-start.2
  4.1 1.0 copy-done.2
  5.1 0.0 copy-start.3
  5.1 0.8 copy-done.3
  5.9 0.0 copy-start.4
  5.9 0.7 copy-done.4
  6.6 0.0 copy-start.5
  6.6 0.7 copy-done.5
  7.3 97.3 %shard_map.103 = (bf16[2,64,1024]{2,1,0:T(8,128)(2,1)S(1)}, f32[2,64]{1,0:T(2,128)S(1)}, f32[2,64]{1,0:T(2,128)S(1)}) custom-call(bf16[2,64,1024]{2,1,0:T(8,128)(2,1)S(1)} %bitcast.11, bf16[3,1024,1024]{2,1,0:T(8,128)(2,1)} %conv_w_hbm.1, f32[1,1024]{1,0:T(1,128)S(1)} %bitcast.14, bf16[3,1024,256]{2,1,0:T(8,128)(2,1)S(1)} %bitcast.10, ...), custom_call_target="tpu_custom_call" | custom-call | tf_op jit(solution)/shard_map/pallas_call | solution.py:422
  104.6 1.0 copy.12
  105.5 0.6 copy.17
  106.1 0.6 copy.18
Async XLA Ops:
  1.6 1.4 %copy-start = (bf16[1024,3,256]{2,0,1:T(8,128)(2,1)S(1)}, bf16[1024,3,256]{2,0,1:T(8,128)(2,1)}, u32[]{:S(2)}) copy-start(bf16[1024,3,256]{2,0,1:T(8,128)(2,1)} %param.11) | copy-start | bytes 4718596
  3.0 1.0 copy-start.1
  4.1 1.0 copy-start.2
  5.1 0.8 copy-start.3
  5.9 0.7 copy-start.4
  6.6 0.7 copy-start.5

commit v2 on v1

--- a/solution.py
+++ b/solution.py
@@ -22,9 +22,9 @@
 
 def encoder_kernel(
     n_f, n_c, n_h,
-    video_ref, conv_w_hbm, gain_ref, qkv_w_hbm, out_w_hbm, latent_w_ref, codes_hbm, wanted_ref,
+    video_hbm, conv_w_hbm, gain_hbm, qkv_w_hbm, out_w_hbm, latent_w_hbm, codes_hbm, wanted_hbm,
     encoded_ref, least_ref, gap_ref,
-    ext, conv_w, mixed, block_input, normed, qkv_w, queries, kv, top, denom, summed,
+    gain_ref, latent_w_ref, wanted_ref, ext, conv_w, mixed, block_input, normed, qkv_w, queries, kv, top, denom, summed,
     attended, gathered, out_w, codes, augmented, lhs, wanted,
     local_sems, send_sems, recv_sems, kv_send, kv_recv, halo_send, halo_recv,
 ):
@@ -33,7 +33,7 @@
     c = lax.axis_index("code")
     h = lax.axis_index("head")
     g = c * n_h + h
-    fh, pos, width = video_ref.shape
+    fh, pos, width = video_hbm.shape
     rows = fh * pos
     chip_rows = n_h * rows
     lw = out_w_hbm.shape[0]
@@ -52,7 +52,12 @@
     qkv_copy = pltpu.make_async_copy(qkv_w_hbm, qkv_w, local_sems.at[3])
     out_copy = pltpu.make_async_copy(out_w_hbm, out_w.at[g], local_sems.at[4])
     codes_copy = pltpu.make_async_copy(codes_hbm, codes.at[g], local_sems.at[5])
-    for copy in [codes_copy] + conv_copies + [qkv_copy, out_copy]:
+    video_copy = pltpu.make_async_copy(video_hbm, ext.at[pl.ds(2, fh)], local_sems.at[6])
+    gain_copy = pltpu.make_async_copy(gain_hbm, gain_ref, local_sems.at[7])
+    latent_w_copy = pltpu.make_async_copy(latent_w_hbm, latent_w_ref, local_sems.at[8])
+    wanted_copy = pltpu.make_async_copy(wanted_hbm, wanted_ref, local_sems.at[9])
+    small_copies = [gain_copy, latent_w_copy, wanted_copy]
+    for copy in [codes_copy, video_copy] + conv_copies + [qkv_copy, out_copy] + small_copies:
         copy.start()
 
     barrier = pltpu.get_barrier_semaphore()
@@ -71,7 +76,7 @@
     pl.semaphore_wait(barrier, n_g - 1 + n_f - 1)
 
     halo = pltpu.make_async_remote_copy(
-        src_ref=video_ref.at[pl.ds(fh - 2, 2)],
+        src_ref=video_hbm.at[pl.ds(fh - 2, 2)],
         dst_ref=ext.at[pl.ds(0, 2)],
         send_sem=halo_send,
         recv_sem=halo_recv,
@@ -138,7 +143,7 @@
     codes_copy.wait()
     spread(0, codes_block)
 
-    ext[2:] = video_ref[...]
+    video_copy.wait()
     tile = tile_of(width, 256)
 
     def tap(k):
@@ -166,8 +171,10 @@
 
     tap(1)
     tap(2)
+    for copy in small_copies:
+        copy.wait()
     conv = mixed[...]
-    values = (video_ref[...].reshape(rows, width).astype(F32) + conv / (1.0 + jnp.exp(-conv))).astype(BF16)
+    values = (ext[2:].reshape(rows, width).astype(F32) + conv / (1.0 + jnp.exp(-conv))).astype(BF16)
     block_input[...] = values
     values32 = values.astype(F32)
     mean_square = jnp.mean(values32 * values32, axis=-1, keepdims=True)
@@ -187,33 +194,37 @@
                 if kind == 0:
                     queries[p, at, :] = piece * (1.0 / math.sqrt(head_dim))
                 else:
-                    kv[fr, kind - 1, p, at, :] = piece
+                    kv[fr, c2, kind - 1, p] = piece
+
+    def kv_copy(slot, c2, df):
+        return pltpu.make_async_remote_copy(
+            src_ref=kv.at[slot, c2],
+            dst_ref=kv.at[slot, c2],
+            send_sem=kv_send.at[df, c2],
+            recv_sem=kv_recv.at[slot, c2],
+            device_id={"frames": lax.rem(fr + df, n_f)},
+            device_id_type=MESH,
+        )
+
+    def send_kv(c2):
+        for df in reversed(range(1, n_f)):
+            @pl.when(fr + df < n_f)
+            def _():
+                kv_copy(fr, c2, df).start()
 
     qkv_copy.wait()
     rest(1, normed_block, 0)
     project(c)
+    send_kv(c)
     for dc in range(1, n_c):
         forward(1, normed_block, dc)
     out_copy.wait()
     spread(2, out_block)
     for dc in range(1, n_c):
         rest(1, normed_block, dc)
-        project(lax.rem(c + n_c - dc, n_c))
-
-    def kv_copy(slot, df):
-        return pltpu.make_async_remote_copy(
-            src_ref=kv.at[slot],
-            dst_ref=kv.at[slot],
-            send_sem=kv_send.at[df],
-            recv_sem=kv_recv.at[slot],
-            device_id={"frames": lax.rem(fr + df, n_f)},
-            device_id_type=MESH,
-        )
-
-    for df in range(1, n_f):
-        @pl.when(fr + df < n_f)
-        def _():
-            kv_copy(fr, df).start()
+        other = lax.rem(c + n_c - dc, n_c)
+        project(other)
+        send_kv(other)
 
     q_tile = tile_of(slab, 256)
     lane = lax.broadcasted_iota(jnp.int32, (q_tile, LANES), 1) // head_dim
@@ -231,8 +242,8 @@
             first = (step % (slab // q_tile)) * q_tile
             at = pl.ds(pl.multiple_of(first, q_tile), q_tile)
             q = queries[p, at, :]
-            k = kv[slot, 0, p]
-            v = kv[slot, 1, p]
+            k = kv[slot, :, 0, p].reshape(slab, LANES)
+            v = kv[slot, :, 1, p].reshape(slab, LANES)
             if own:
                 q_row = first + lax.broadcasted_iota(jnp.int32, (q_tile, slab), 0)
                 k_row = lax.broadcasted_iota(jnp.int32, (q_tile, slab), 1)
@@ -271,7 +282,7 @@
         forward(0, codes_block, dc)
     for dc in range(n_c):
         rest(0, codes_block, dc)
-    c_tile = tile_of(shard, 1024)
+    c_tile = tile_of(shard, 8192)
 
     @pl.loop(0, n_g * (shard // c_tile))
     def _(step):
@@ -294,8 +305,9 @@
         rest(2, out_block, dc)
 
     def visit(k, carry):
-        slot = fr - 1 - k
-        kv_copy(slot, 1).wait_recv()
+        slot = k
+        for part in range(n_c):
+            kv_copy(slot, part, 1).wait_recv()
         absorb(slot, False)
         return carry
 
@@ -402,7 +414,8 @@
     for df in range(1, n_f):
         @pl.when(fr + df < n_f)
         def _():
-            kv_copy(fr, df).wait_send()
+            for part in range(n_c):
+                kv_copy(fr, part, df).wait_send()
 
 
 def shards(
@@ -418,7 +431,7 @@
     code_dim, shard = codebook.shape
     sends = 3 * (n_c - 1 + n_h - 1 + (n_c - 1) * (n_h - 1)) + n_g - 1
     vmem = pl.BlockSpec(memory_space=pltpu.VMEM)
-    anywhere = pl.BlockSpec(memory_space=pl.ANY)
+    hbm = pl.BlockSpec(memory_space=pltpu.HBM)
     encoded, least, gap = pl.pallas_call(
         functools.partial(encoder_kernel, n_f, n_c, n_h),
         out_shape=(
@@ -426,9 +439,12 @@
             jax.ShapeDtypeStruct((frames_here, positions), F32),
             jax.ShapeDtypeStruct((frames_here, positions), F32),
         ),
-        in_specs=[vmem, anywhere, vmem, anywhere, anywhere, vmem, anywhere, vmem],
+        in_specs=[hbm] * 8,
         out_specs=(vmem, vmem, vmem),
         scratch_shapes=[
+            pltpu.VMEM((1, width), F32),
+            pltpu.VMEM((code_dim, width), BF16),
+            pltpu.VMEM((frames_here, reference_codes.shape[0]), jnp.int32),
             pltpu.VMEM((2 + frames_here, positions, width), BF16),
             pltpu.VMEM(conv_weight.shape, BF16),
             pltpu.VMEM((rows, width), F32),
@@ -436,7 +452,7 @@
             pltpu.VMEM((slab, width), BF16),
             pltpu.VMEM((3, width, lw), BF16),
             pltpu.VMEM((pairs, slab, LANES), BF16),
-            pltpu.VMEM((n_f, 2, pairs, slab, LANES), BF16),
+            pltpu.VMEM((n_f, n_c, 2, pairs, n_h * rows, LANES), BF16),
             pltpu.VMEM((pairs, slab, LANES), F32),
             pltpu.VMEM((pairs, slab, LANES), F32),
             pltpu.VMEM((pairs, slab, LANES), F32),
@@ -447,11 +463,11 @@
             pltpu.VMEM((n_g, 2 * code_dim, shard), BF16),
             pltpu.VMEM((rows, 2 * code_dim), F32),
             pltpu.VMEM((rows, LANES), jnp.int32),
-            pltpu.SemaphoreType.DMA((6,)),
+            pltpu.SemaphoreType.DMA((10,)),
             pltpu.SemaphoreType.DMA((sends,)),
             pltpu.SemaphoreType.DMA((4, n_g)),
-            pltpu.SemaphoreType.DMA((n_f,)),
-            pltpu.SemaphoreType.DMA((n_f,)),
+            pltpu.SemaphoreType.DMA((n_f, n_c)),
+            pltpu.SemaphoreType.DMA((n_f, n_c)),
             pltpu.SemaphoreType.DMA,
             pltpu.SemaphoreType.DMA,
         ],

time: 107 us -> 82.4 us (0.77)
  the two profiles are of different devices: /device:TPU:31 before, /device:TPU:16 now
where the time goes in v2:
time: 82.4 us; the launch traced here: 82 us
  Pallas kernels  72.6 us (88%)
  local copies, waits for them, and re-layouts  8.7 us (11%)
    pallas_call x1, Pallas kernels, shards(): pl.pallas_call(functools.partial(encoder_kernel, n_f, n_c, n_h), out_shap...  72.6 us
    unnamed x16, local copies, waits for them, and re-layouts  8.7 us

profile of v2, /device:TPU:16, one launch (start us, length us, event | category | flops | bytes accessed | tf_op | source)
XLA Modules:
  0.0 82.0 jit_solution(15768983666194999896)
XLA Ops:
  0.6 1.0 %copy.14 = bf16[64,2,1024]{2,0,1:T(8,128)(2,1)S(1)} copy(bf16[64,2,1024]{2,1,0:T(2,128)(2,1)} %param.8) | data formatting | bytes 524288 | tf_op args[0]
  1.6 0.0 copy-start
  1.6 1.4 %copy-done = bf16[1024,3,256]{2,0,1:T(8,128)(2,1)S(1)} copy-done((bf16[1024,3,256]{2,0,1:T(8,128)(2,1)S(1)}, bf16[1024,3,256]{2,0,1:T(8,128)(2,1)}, u32[]{:S(2)}) %copy-start) | copy-done | bytes 1572888
  3.0 0.0 copy-start.1
  3.0 1.0 %copy-done.1 = bf16[256,1024]{1,0:T(8,128)(2,1)S(1)} copy-done((bf16[256,1024]{1,0:T(8,128)(2,1)S(1)}, bf16[256,1024]{1,0:T(8,128)(2,1)}, u32[]{:S(2)}) %copy-start.1) | copy-done | bytes 524312
  4.1 0.0 copy-start.2
  4.1 1.0 %copy-done.2 = bf16[16,16384]{1,0:T(8,128)(2,1)S(1)} copy-done((bf16[16,16384]{1,0:T(8,128)(2,1)S(1)}, bf16[16,16384]{1,0:T(8,128)(2,1)}, u32[]{:S(2)}) %copy-start.2) | copy-done | bytes 524312
  5.1 0.0 copy-start.3
  5.1 0.8 copy-done.3
  5.9 0.0 copy-start.4
  5.9 0.7 copy-done.4
  6.6 0.0 copy-start.5
  6.6 0.7 copy-done.5
  7.3 72.6 %shard_map.103 = (bf16[2,64,1024]{2,1,0:T(8,128)(2,1)S(1)}, f32[2,64]{1,0:T(2,128)S(1)}, f32[2,64]{1,0:T(2,128)S(1)}) custom-call(bf16[2,64,1024]{2,1,0:T(8,128)(2,1)S(1)} %bitcast.11, bf16[3,1024,1024]{2,1,0:T(8,128)(2,1)} %conv_w_hbm.1, f32[1,1024]{1,0:T(1,128)S(1)} %bitcast.14, bf16[3,1024,256]{2,1,0:T(8,128)(2,1)S(1)} %bitcast.10, ...), custom_call_target="tpu_custom_call" | custom-call | tf_op jit(solution)/shard_map/pallas_call | solution.py:435
  79.9 1.0 %copy.12 = bf16[64,2,1024]{2,1,0:T(2,128)(2,1)} copy(bf16[64,2,1024]{2,0,1:T(8,128)(2,1)S(1)} %bitcast.12) | data formatting | bytes 524288
  80.8 0.6 copy.17
  81.4 0.6 copy.18
Async XLA Ops:
  1.6 1.4 %copy-start = (bf16[1024,3,256]{2,0,1:T(8,128)(2,1)S(1)}, bf16[1024,3,256]{2,0,1:T(8,128)(2,1)}, u32[]{:S(2)}) copy-start(bf16[1024,3,256]{2,0,1:T(8,128)(2,1)} %param.11) | copy-start | bytes 4718596
  3.0 1.0 %copy-start.1 = (bf16[256,1024]{1,0:T(8,128)(2,1)S(1)}, bf16[256,1024]{1,0:T(8,128)(2,1)}, u32[]{:S(2)}) copy-start(bf16[256,1024]{1,0:T(8,128)(2,1)} %out_w_hbm.1) | copy-start | bytes 1572868
  4.1 1.0 %copy-start.2 = (bf16[16,16384]{1,0:T(8,128)(2,1)S(1)}, bf16[16,16384]{1,0:T(8,128)(2,1)}, u32[]{:S(2)}) copy-start(bf16[16,16384]{1,0:T(8,128)(2,1)} %codes_hbm.1) | copy-start | bytes 1572868
  5.1 0.8 copy-start.3
  5.9 0.7 copy-start.4
  6.6 0.7 copy-start.5

commit v3 on v2

--- a/solution.py
+++ b/solution.py
@@ -144,7 +144,7 @@
     spread(0, codes_block)
 
     video_copy.wait()
-    tile = tile_of(width, 256)
+    tile = tile_of(width, 1024)
 
     def tap(k):
         conv_copies[k].wait()
@@ -472,7 +472,7 @@
             pltpu.SemaphoreType.DMA,
         ],
         compiler_params=pltpu.CompilerParams(
-            collective_id=0, has_side_effects=True, vmem_limit_bytes=48 * 1024 * 1024
+            collective_id=0, has_side_effects=True, vmem_limit_bytes=60 * 1024 * 1024
         ),
     )(
         jnp.transpose(video, (1, 0, 2)),

time: 82.4 us -> 79 us (0.959)
  local copies, waits for them, and re-layouts: 8.7 us -> 6.09 us
    unnamed x16 -> x4, local copies, waits for them, and re-layouts: 8.7 us -> 6.09 us
where the time goes in v3:
time: 79 us; the launch traced here: 78.8 us
  Pallas kernels  72.1 us (91%)
  local copies, waits for them, and re-layouts  6.09 us (8%)
    pallas_call x1, Pallas kernels, shards(): pl.pallas_call(functools.partial(encoder_kernel, n_f, n_c, n_h), out_shap...  72.1 us
    unnamed x4, local copies, waits for them, and re-layouts  6.09 us

profile of v3, /device:TPU:16, one launch (start us, length us, event | category | flops | bytes accessed | tf_op | source)
XLA Modules:
  0.0 78.8 jit_solution(12295706057000809731)
XLA Ops:
  0.6 1.7 %copy.14 = bf16[64,2,1024]{2,0,1:T(8,128)(2,1)} copy(bf16[64,2,1024]{2,1,0:T(2,128)(2,1)} %param.8) | data formatting | bytes 524288 | tf_op args[0]
  2.3 72.1 %shard_map.103 = (bf16[2,64,1024]{2,1,0:T(8,128)(2,1)}, f32[2,64]{1,0:T(2,128)}, f32[2,64]{1,0:T(2,128)}) custom-call(bf16[2,64,1024]{2,1,0:T(8,128)(2,1)} %bitcast.11, bf16[3,1024,1024]{2,1,0:T(8,128)(2,1)} %conv_w_hbm.1, f32[1,1024]{1,0:T(1,128)} %bitcast.14, bf16[3,1024,256]{2,1,0:T(8,128)(2,1)} %bitcast.10, bf16[256,1024]{1,0:T(8,128)(2,1)} %out_w_hbm.1, ...), custom_call_target="tpu_custom_call" | custom-call | tf_op jit(solution)/shard_map/pallas_call | solution.py:435
  74.4 1.9 %copy.12 = bf16[64,2,1024]{2,1,0:T(2,128)(2,1)} copy(bf16[64,2,1024]{2,0,1:T(8,128)(2,1)} %bitcast.12) | data formatting | bytes 524288
  76.3 1.2 %copy.17 = f32[64,2]{0,1:T(2,128)} copy(f32[64,2]{0,1:T(2,128)} %bitcast.17) | data formatting | bytes 1024
  77.6 1.2 %copy.18 = f32[64,2]{0,1:T(2,128)} copy(f32[64,2]{0,1:T(2,128)} %bitcast.16) | data formatting | bytes 1024
